TPU v7x, 32 devices: a whole 2x2x4 slice. The times are simulated.
32 devices in a mesh: expert: 8 (over z, x), tensor: 4 (over y, core).
Axes of the slice: x: 2, y: 2, z: 4, core: 2. Of those that a mesh axis runs over, the one named last changes fastest.
Arguments:
- routes: int32 [1024, 2], P('expert'), may hold values from 0 to 7, all different within a row; in each aligned block of 128 rows (0 to 127, 128 to 255, ...) at most 40 rows name the same one
- gate_weights: float32 [1024, 2], P('expert'), may hold values from 0.2 to 1
- out_grad: bfloat16 [1024, 3072], P('expert', 'tensor'), may hold values from -6 to 6
- hidden: bfloat16 [8, 320, 6144], P('expert', None, 'tensor'), may hold values from -6 to 6
- down_weight: bfloat16 [8, 6144, 3072], P('expert', 'tensor'), may hold values from -0.078125 to 0.078125
Outputs:
- layer_out: bfloat16 [1024, 3072], P('expert', 'tensor')
- gate_grad: float32 [1024, 2], P('expert')
- hidden_grad: bfloat16 [8, 320, 6144], P('expert', None, 'tensor')
Inputs may be any that keep to these rules, and one draw needn't show every extreme that they name: `routes`: each row names 2 different experts. Among the 128 x 2 entries of the rows of one device, no expert is named more than 40 times, a bound that some block reaches there.
All inputs are finite; a program needn't handle non-finite values.
Results may differ from a plain program's by a relative error of at most 0.0051.
Values may be sent and summed in bfloat16 or wider, within the bound.
A program may use at most 64 MiB of HBM per device.

v0:
```python
import jax
import jax.numpy as jnp
from jax import lax
from jax.sharding import PartitionSpec as P


def per_device(routes, gate_weights, out_grad, hidden, down_weight):
    sources = lax.axis_size("expert")
    slots = hidden.shape[1]
    capacity = slots // sources
    weight = down_weight[0]
    flat = routes.reshape(-1)
    onehot = (flat[:, None] == jnp.arange(sources, dtype=jnp.int32)[None, :]).astype(jnp.int32)
    position = jnp.sum((jnp.cumsum(onehot, axis=0) - onehot) * onehot, axis=1)
    column = (flat * capacity + position).reshape(routes.shape)
    marks = column[:, :, None] == jnp.arange(slots, dtype=jnp.int32)[None, None, :]
    marks_half = marks.astype(jnp.bfloat16)
    picker = jnp.sum(marks.astype(jnp.float32), axis=1).astype(jnp.bfloat16)
    slot_gate = jnp.sum(gate_weights[:, :, None] * marks.astype(jnp.float32), axis=(0, 1))
    columns = weight
    summed = lax.psum_scatter(
        lax.dot_general(
            columns, hidden[0], (((0,), (1,)), ((), ())), preferred_element_type=jnp.float32
        ),
        "tensor",
        scatter_dimension=0,
        tiled=True,
    )
    outgoing = summed.astype(jnp.bfloat16)
    picked = lax.dot_general(
        out_grad, picker, (((0,), (0,)), ((), ())), preferred_element_type=jnp.float32
    )
    to_send = (picked * slot_gate[None, :]).astype(jnp.bfloat16)
    returned = lax.all_to_all(outgoing, "expert", split_axis=1, concat_axis=1, tiled=True)
    arrived = lax.all_to_all(to_send, "expert", split_axis=1, concat_axis=1, tiled=True)
    chosen = lax.dot_general(
        marks_half, returned, (((2,), (1,)), ((), ())), preferred_element_type=jnp.float32
    )
    layer_out = jnp.sum(gate_weights[:, :, None] * chosen, axis=1).astype(jnp.bfloat16)
    own_terms = jnp.sum(out_grad.astype(jnp.float32)[:, None, :] * chosen, axis=2)
    gate_grad = lax.psum(own_terms, "tensor")
    columns = weight
    grad_sum = lax.dot_general(
        lax.all_gather(arrived, "tensor", axis=0, tiled=True),
        columns,
        (((0,), (1,)), ((), ())),
        preferred_element_type=jnp.float32,
    )
    hidden_grad = grad_sum.astype(jnp.bfloat16)[None]
    return (layer_out, gate_grad, hidden_grad)


def solution(mesh):
    return jax.shard_map(
        per_device,
        mesh=mesh,
        in_specs=(
            P("expert", None),
            P("expert", None),
            P("expert", "tensor"),
            P("expert", None, "tensor"),
            P("expert", "tensor", None),
        ),
        out_specs=(P("expert", "tensor"), P("expert", None), P("expert", None, "tensor")),
        check_vma=False,
    )
```

profile of v0, /device:TPU:0, one launch (start us, length us, event | category | flops | bytes accessed | tf_op | source)
XLA Modules:
  0.0 109.4 jit_solution(8269657567912467484)
XLA Ops:
  7.2 0.0 reduce-scatter.2.cloned.1.call-start
  7.3 1.1 %copy-done = bf16[1,320,1536]{2,1,0:T(8,128)(2,1)S(1)} copy-done((bf16[1,320,1536]{2,1,0:T(8,128)(2,1)S(1)}, bf16[1,320,1536]{2,1,0:T(8,128)(2,1)}, u32[]{:S(2)}) %copy-start) | copy-done | bytes 983064
  8.4 8.8 %fusion.2 = f32[3072,320]{0,1:T(8,128)} fusion(bf16[1,1536,3072]{2,1,0:T(8,128)(2,1)} %param.9, bf16[1,320,1536]{2,1,0:T(8,128)(2,1)S(1)} %copy-done), kind=kOutput, calls=%fused_computation.2 | convolution fusion | flops 3019898880 | bytes 14352384 | tf_op jit(solution)/shard_map/dot_general | solution.py:22
  17.1 0.0 reduce-scatter.2.cloned.1.call-update
  17.2 0.0 all-gather.2.cloned.1.call-start
  17.2 0.1 copy.18
  17.3 0.1 eq.42
  17.5 0.1 eq.38
  17.6 0.6 reduce-window.6
  18.2 0.2 slice_reduce_fusion
  18.5 0.1 fusion.16
  18.6 0.1 reduce_sum.48
  18.7 0.1 copy.20
  18.8 0.2 convert_reduce_fusion
  19.0 0.3 fusion.10
  19.3 21.0 %all_to_all.24 = bf16[768,8,40]{0,2,1:T(8,128)(2,1)} all-to-all(bf16[768,8,40]{0,2,1:T(8,128)(2,1)S(1)} %bitcast.35), channel_id=1, replica_groups=mesh['expert'=8,'tensor'=4] {'expert'}, dimensions={1} | all-to-all | bytes 983040 | tf_op jit(solution)/shard_map/all_to_all | solution.py:35
  40.2 0.0 all-gather.2.cloned.1.call-update
  40.3 22.6 %reduce-scatter.2.cloned.1.call-done = f32[768,320]{0,1:T(8,128)} async-done(((f32[3072,320]{0,1:T(8,128)}), f32[768,320]{0,1:T(8,128)}) %reduce-scatter.2.cloned.1.call-update) | async-done | bytes 983056 | tf_op jit(solution)/shard_map/reduce_scatter | solution.py:21
  62.9 2.0 %convert_element_type.35 = bf16[768,320]{0,1:T(8,128)(2,1)} convert(f32[768,320]{0,1:T(8,128)} %reduce-scatter.2.cloned.1.call-done) | non-fusion elementwise | flops 245760 | bytes 1474560 | tf_op jit(solution)/shard_map/convert_element_type | solution.py:29
  64.9 5.5 %all-to-all-start = ((bf16[768,8,40]{0,2,1:T(8,128)(2,1)}), bf16[768,8,40]{0,2,1:T(8,128)(2,1)S(1)}, u32[]{:S(2)}, u32[]{:S(2)}) async-start(bf16[768,8,40]{0,2,1:T(8,128)(2,1)} %bitcast.4), calls=%async_computation.1 | async-start | bytes 983040 | tf_op jit(solution)/shard_map/all_to_all | solution.py:34
  70.4 16.0 %all-gather.2.cloned.1.call-done = bf16[3072,320]{0,1:T(8,128)(2,1)} async-done(((bf16[768,320]{0,1:T(8,128)(2,1)}), bf16[3072,320]{0,1:T(8,128)(2,1)}) %all-gather.2.cloned.1.call-update) | async-done | bytes 1966096 | tf_op jit(solution)/shard_map/all_gather | solution.py:44
  86.4 8.5 %fusion.7 = bf16[1,320,1536]{2,1,0:T(8,128)(2,1)} fusion(bf16[3072,320]{0,1:T(8,128)(2,1)} %all-gather.2.cloned.1.call-done, bf16[1,1536,3072]{2,1,0:T(8,128)(2,1)} %param.9), kind=kOutput, calls=%fused_computation.5 | convolution fusion | flops 3020390400 | bytes 12386304 | tf_op jit(solution)/shard_map/dot_general | solution.py:43
  94.9 1.2 %multiply_reduce_fusion = (f32[128,2]{0,1:T(2,128)S(1)}, bf16[128,768]{1,0:T(8,128)(2,1)}) fusion(f32[128,768]{1,0:T(8,128)S(1)} %convert_element_type.37, f32[128,2]{0,1:T(2,128)S(1)} %copy-done.3, bf16[768,320,1]{0,1,2:T(8,128)(2,1)S(1)} %bitcast.36, s32[128,2]{0,1:T(2,128)S(1)} %multiply_add_fusion), kind=kOutput, calls=%fused_computation.9 | convolution fusion | flops 126598912 | bytes 1084416 | tf_op jit(solution)/shard_map/dot_general | solution.py:36
  96.1 6.4 %psum.7 = f32[128,2]{0,1:T(2,128)} all-reduce(f32[128,2]{0,1:T(2,128)S(1)} %get-tuple-element.3), channel_id=1, replica_groups=mesh['expert'=8,'tensor'=4] {'tensor'}, use_global_device_ids=true, to_apply=%region_6.7 | all-reduce | flops 256 | bytes 2048 | tf_op jit(solution)/shard_map/psum | solution.py:41
  (13 shorter events, 0.1 us)
Async XLA Ops:
  7.2 1.2 %copy-start = (bf16[1,320,1536]{2,1,0:T(8,128)(2,1)S(1)}, bf16[1,320,1536]{2,1,0:T(8,128)(2,1)}, u32[]{:S(2)}) copy-start(bf16[1,320,1536]{2,1,0:T(8,128)(2,1)} %param.8) | copy-start | bytes 2949124
  7.2 10.0 %copy-start.2 = (s32[128,2]{0,1:T(2,128)S(1)}, s32[128,2]{0,1:T(2,128)}, u32[]{:S(2)}) copy-start(s32[128,2]{0,1:T(2,128)} %param.5) | copy-start | bytes 3076
  7.2 11.6 %copy-start.3 = (f32[128,2]{0,1:T(2,128)S(1)}, f32[128,2]{0,1:T(2,128)}, u32[]{:S(2)}) copy-start(f32[128,2]{0,1:T(2,128)} %param.6) | copy-start | bytes 3076
  7.2 11.8 %copy-start.1 = (bf16[128,768]{1,0:T(8,128)(2,1)S(1)}, bf16[128,768]{1,0:T(8,128)(2,1)}, u32[]{:S(2)}) copy-start(bf16[128,768]{1,0:T(8,128)(2,1)} %param.7) | copy-start | bytes 589828
  7.2 55.7 %reduce-scatter.2.cloned.1.call-start = ((), (), s32[]{:S(2)}) async-start(), calls=%async_computation.3 | async-start | bytes 4915200 | tf_op jit(solution)/shard_map/reduce_scatter | solution.py:21
  17.2 69.3 %all-gather.2.cloned.1.call-start = ((), (), s32[]{:S(2)}) async-start(), calls=%async_computation.4 | async-start | bytes 2457600 | tf_op jit(solution)/shard_map/all_gather | solution.py:44
  64.9 30.0 %all-to-all-start = ((bf16[768,8,40]{0,2,1:T(8,128)(2,1)}), bf16[768,8,40]{0,2,1:T(8,128)(2,1)S(1)}, u32[]{:S(2)}, u32[]{:S(2)}) async-start(bf16[768,8,40]{0,2,1:T(8,128)(2,1)} %bitcast.4), calls=%async_computation.1 | async-start | bytes 983040 | tf_op jit(solution)/shard_map/all_to_all | solution.py:34
Sparse Core Ops, SparseCore 0:
  17.3 45.5 reduce-scatter.1
  64.6 21.8 all-gather.1
where the time goes:
time: 110 us; the launch traced here: 109 us
  waiting for transfers between devices  38.7 us (35%)
  blocking collectives  27.4 us (25%)
  matrix products  18.7 us (17%)
  between operations  14.1 us (13%)
  starting transfers between devices  5.57 us (5%)
  other arithmetic  2.95 us (3%)
  local copies, waits for them, and re-layouts  1.95 us (2%)
    reduce_scatter x1, waiting for transfers between devices, per_device(): lax.psum_scatter(lax.dot_general(columns, hidden[0], (((0,), (1,)), ((),...  22.6 us
    all_to_all x1, blocking collectives, per_device(): lax.all_to_all(to_send, 'expert', split_axis=1, concat_axis=1, tiled=True)  21 us
    all_gather x1, waiting for transfers between devices, per_device(): lax.all_gather(arrived, 'tensor', axis=0, tiled=True)  16 us
    dot_general x1, matrix products, per_device(): lax.dot_general(columns, hidden[0], (((0,), (1,)), ((), ())), preferred_e...  8.76 us
    dot_general x1, matrix products, per_device(): lax.dot_general(lax.all_gather(arrived, 'tensor', axis=0, tiled=True), co...  8.47 us
    psum x1, blocking collectives, per_device(): gate_grad = lax.psum(own_terms, 'tensor')  6.4 us
    all_to_all x1, starting transfers between devices, per_device(): lax.all_to_all(outgoing, 'expert', split_axis=1, concat_axis=1, tiled=True)  5.49 us
  transfers between devices with their start and end apart: 3, of which 2 were waited for; matrix products, arithmetic and copies ran while one was open for 11% of the time, Pallas kernels for 0%

commit v1 on v0

--- a/solution.py
+++ b/solution.py
@@ -1,10 +1,16 @@
 import jax
 import jax.numpy as jnp
 from jax import lax
+from jax.experimental import pallas as pl
+from jax.experimental.pallas import tpu as pltpu
 from jax.sharding import PartitionSpec as P
 
-
-def per_device(routes, gate_weights, out_grad, hidden, down_weight):
+BF16, F32 = jnp.bfloat16, jnp.float32
+FAR_FIRST = (4, 3, 5, 2, 6, 1, 7, 0)
+NEAR_FIRST = (0, 1, 7, 2, 6, 3, 5, 4)
+
+
+def plain(routes, gate_weights, out_grad, hidden, down_weight):
     sources = lax.axis_size("expert")
     slots = hidden.shape[1]
     capacity = slots // sources
@@ -50,6 +56,241 @@
     return (layer_out, gate_grad, hidden_grad)
 
 
+def fused_kernel(
+    routes_ref, gates_ref, out_grad_ref, hidden_hbm, weight_hbm,
+    layer_ref, gate_grad_ref, hidden_grad_ref,
+    hidden, weight, partial, core_out, core_in, y_out, y_in,
+    slots_out, returned, tokens_out, gathered, total, terms,
+    load_sem, core_send, core_recv, y_send, y_recv, out_send, out_recv,
+    tok_send, tok_recv, gc_send, gc_recv, gy_send, gy_recv, gf_send, gf_recv,
+    term_send, term_recv,
+):
+    experts, rows2, half = returned.shape
+    cap = rows2 // 2
+    slots = experts * cap
+    own = lax.axis_index("expert")
+    rank = lax.axis_index("tensor")
+    chip, core = rank // 2, rank % 2
+    sibling = chip * 2 + (1 - core)
+    across = (1 - chip) * 2 + core
+    diagonal = (1 - chip) * 2 + (1 - core)
+    width = 2 * half
+
+    def send(source, target, send_sem, recv_sem, expert, tensor):
+        return pltpu.make_async_remote_copy(
+            src_ref=source, dst_ref=target, send_sem=send_sem, recv_sem=recv_sem,
+            device_id=(expert, tensor), device_id_type=pl.DeviceIdType.MESH,
+        )
+
+    loads = [pltpu.make_async_copy(hidden_hbm.at[0], hidden, load_sem.at[4])]
+    for j, group in enumerate((diagonal, across, sibling, rank)):
+        columns = pl.ds(pl.multiple_of(group * width, width), width)
+        loads.append(pltpu.make_async_copy(
+            weight_hbm.at[0, :, columns], weight.at[j], load_sem.at[j]))
+    for load in loads:
+        load.start()
+
+    barrier = pltpu.get_barrier_semaphore()
+    for i in range(1, experts):
+        pl.semaphore_signal(barrier, inc=1, device_id=((own + i) % experts, rank),
+                            device_id_type=pl.DeviceIdType.MESH)
+    for peer in (sibling, across, diagonal):
+        pl.semaphore_signal(barrier, inc=1, device_id=(own, peer),
+                            device_id_type=pl.DeviceIdType.MESH)
+
+    def pack(values):
+        left = values[:, :half].reshape(experts, cap, half)
+        right = values[:, half:].reshape(experts, cap, half)
+        return jnp.concatenate([left, right], axis=1)
+
+    def unpack(values):
+        values = values.astype(F32)
+        both = jnp.concatenate([values[:, :cap], values[:, cap:]], axis=2)
+        return both.reshape(slots, width).astype(BF16)
+
+    routes = routes_ref[...]
+    gates = gates_ref[...]
+    tokens = routes.shape[1]
+    expert_id = lax.broadcasted_iota(jnp.int32, (experts, tokens), 0)
+    named = [(expert_id == routes[k:k + 1]).astype(F32) for k in range(2)]
+    earlier = (lax.broadcasted_iota(jnp.int32, (tokens, tokens), 0)
+               < lax.broadcasted_iota(jnp.int32, (tokens, tokens), 1))
+    before = jnp.dot((named[0] + named[1]).astype(BF16), earlier.astype(F32).astype(BF16),
+                     preferred_element_type=F32)
+    slot_id = lax.broadcasted_iota(jnp.int32, (slots, tokens), 0)
+    marks = []
+    for k in range(2):
+        position = jnp.sum(before * named[k], axis=0, keepdims=True).astype(jnp.int32)
+        marks.append((slot_id == routes[k:k + 1] * cap + position).astype(F32))
+    slot_gate = jnp.sum(marks[0] * gates[0:1] + marks[1] * gates[1:2], axis=1, keepdims=True)
+    picked = jnp.dot((marks[0] + marks[1]).astype(BF16), out_grad_ref[...],
+                     preferred_element_type=F32)
+    tokens_out[...] = pack(picked * slot_gate).astype(BF16)
+
+    pl.semaphore_wait(barrier, experts - 1 + 3)
+
+    sends = []
+    token_copies = {}
+    for i in FAR_FIRST[:-1]:
+        expert = (own + i) % experts
+        token_copies[i] = send(tokens_out.at[expert], gathered.at[0, own],
+                               tok_send.at[i], tok_recv.at[i], expert, rank)
+        token_copies[i].start()
+    gathered[0, own] = tokens_out[own]
+
+    def product(j):
+        return pack(jnp.dot(hidden[...], weight[j], preferred_element_type=F32))
+
+    loads[0].wait()
+    loads[1].wait()
+    core_out[0] = product(0).astype(BF16)
+    to_core = [send(core_out.at[n], core_in.at[n], core_send.at[n], core_recv.at[n], own, sibling)
+               for n in range(2)]
+    to_core[0].start()
+    loads[2].wait()
+    partial[...] = product(1)
+    to_core[0].wait_recv()
+    to_y = {}
+    for i in FAR_FIRST:
+        expert = (own + i) % experts
+        y_out[expert] = (partial[expert] + core_in[0, expert].astype(F32)).astype(BF16)
+        to_y[i] = send(y_out.at[expert], y_in.at[expert], y_send.at[i], y_recv.at[i], own, across)
+        to_y[i].start()
+    loads[3].wait()
+    core_out[1] = product(2).astype(BF16)
+    to_core[1].start()
+    loads[4].wait()
+    partial[...] = product(3)
+    to_core[1].wait_recv()
+    partial[...] = partial[...] + core_in[1].astype(F32)
+
+    to_slots, to_sibling, to_across, onward = {}, {}, {}, {}
+    for far, near in zip(FAR_FIRST, NEAR_FIRST):
+        source = (own - near + experts) % experts
+        if near:
+            token_copies[near].wait_recv()
+        to_across[near] = send(gathered.at[0, source], gathered.at[2, source],
+                               gy_send.at[near], gy_recv.at[near], own, across)
+        to_across[near].start()
+        to_sibling[near] = send(gathered.at[0, source], gathered.at[1, source],
+                                gc_send.at[near], gc_recv.at[near], own, sibling)
+        to_sibling[near].start()
+
+        expert = (own + far) % experts
+        to_y[far].wait_recv()
+        block = (partial[expert] + y_in[expert].astype(F32)).astype(BF16)
+        if far:
+            slots_out[expert] = block
+            to_slots[far] = send(slots_out.at[expert], returned.at[own],
+                                 out_send.at[far], out_recv.at[far], expert, rank)
+            to_slots[far].start()
+        else:
+            returned[own] = block
+
+    def back(part, j):
+        return lax.dot_general(unpack(gathered[part]), weight[j], (((1,), (1,)), ((), ())),
+                               preferred_element_type=F32)
+
+    total[...] = back(0, 3)
+    for near in NEAR_FIRST:
+        to_sibling[near].wait_recv()
+    total[...] = total[...] + back(1, 2)
+    for near in NEAR_FIRST:
+        source = (own - near + experts) % experts
+        to_across[near].wait_recv()
+        onward[near] = send(gathered.at[2, source], gathered.at[3, source],
+                            gf_send.at[near], gf_recv.at[near], own, sibling)
+        onward[near].start()
+    total[...] = total[...] + back(2, 1)
+
+    for far in FAR_FIRST[:-1]:
+        to_slots[far].wait_recv()
+    outputs = unpack(returned[...])
+    cotangent = out_grad_ref[...].astype(F32)
+    layer = jnp.zeros((tokens, width), F32)
+    lane = lax.broadcasted_iota(jnp.int32, (tokens, tokens), 1)
+    spread = jnp.zeros((tokens, tokens), F32)
+    for k in range(2):
+        chosen = jnp.dot(marks[k].T.astype(BF16), outputs, preferred_element_type=F32)
+        gate = jnp.broadcast_to(gates[k:k + 1], (tokens, tokens)).T[:, :1]
+        layer = layer + gate * chosen
+        term = jnp.sum(cotangent * chosen, axis=1, keepdims=True)
+        spread = spread + jnp.where(lane == k, term, 0.0)
+    layer_ref[...] = layer.astype(BF16)
+    terms[rank] = spread.T[:8]
+    to_terms = []
+    for n, peer in enumerate((sibling, across, diagonal)):
+        to_terms.append(send(terms.at[rank], terms.at[rank], term_send.at[n], term_recv.at[n],
+                             own, peer))
+        to_terms[n].start()
+
+    for near in NEAR_FIRST:
+        onward[near].wait_recv()
+    hidden_grad_ref[0] = (total[...] + back(3, 0)).astype(BF16)
+
+    for copy in to_terms:
+        copy.wait_recv()
+    gate_grad_ref[...] = (terms[0] + terms[1] + terms[2] + terms[3])[:2]
+
+    for group in (token_copies, to_y, to_slots, to_sibling, to_across, onward):
+        for copy in group.values():
+            copy.wait_send()
+    for copy in to_core + to_terms:
+        copy.wait_send()
+
+
+def fused(routes, gate_weights, out_grad, hidden, down_weight):
+    experts = lax.axis_size("expert")
+    _, slots, depth = hidden.shape
+    tokens, width = out_grad.shape
+    blocks = (experts, 2 * slots // experts, width // 2)
+    vmem = pl.BlockSpec(memory_space=pltpu.VMEM)
+    hbm = pl.BlockSpec(memory_space=pl.ANY)
+    sems = lambda n: pltpu.SemaphoreType.DMA((n,))
+    layer_out, gate_grad, hidden_grad = pl.pallas_call(
+        fused_kernel,
+        out_shape=(
+            jax.ShapeDtypeStruct((tokens, width), BF16),
+            jax.ShapeDtypeStruct((2, tokens), F32),
+            jax.ShapeDtypeStruct((1, slots, depth), BF16),
+        ),
+        in_specs=[vmem, vmem, vmem, hbm, hbm],
+        out_specs=(vmem, vmem, vmem),
+        scratch_shapes=[
+            pltpu.VMEM((slots, depth), BF16),
+            pltpu.VMEM((4, depth, width), BF16),
+            pltpu.VMEM(blocks, F32),
+            pltpu.VMEM((2,) + blocks, BF16),
+            pltpu.VMEM((2,) + blocks, BF16),
+            pltpu.VMEM(blocks, BF16),
+            pltpu.VMEM(blocks, BF16),
+            pltpu.VMEM(blocks, BF16),
+            pltpu.VMEM(blocks, BF16),
+            pltpu.VMEM(blocks, BF16),
+            pltpu.VMEM((4,) + blocks, BF16),
+            pltpu.VMEM((slots, depth), F32),
+            pltpu.VMEM((4, 8, tokens), F32),
+            sems(5), sems(2), sems(2),
+        ] + [sems(8)] * 12 + [sems(3), sems(3)],
+        compiler_params=pltpu.CompilerParams(
+            collective_id=0, has_side_effects=True, vmem_limit_bytes=56 * 1024 * 1024
+        ),
+        cost_estimate=pl.CostEstimate(
+            flops=16 * slots * depth * width, bytes_accessed=8 * depth * width, transcendentals=0
+        ),
+    )(routes.T, gate_weights.T, out_grad, hidden, down_weight)
+    return layer_out, gate_grad.T, hidden_grad
+
+
+def per_device(routes, gate_weights, out_grad, hidden, down_weight):
+    experts, ranks = lax.axis_size("expert"), lax.axis_size("tensor")
+    cap = hidden.shape[1] // experts
+    fits = (experts == 8 and ranks == 4 and cap % 8 == 0 and routes.shape == (128, 2)
+            and out_grad.shape[1] % 256 == 0 and hidden.shape[2] % 128 == 0)
+    chosen = fused if fits else plain
+    return chosen(routes, gate_weights, out_grad, hidden, down_weight)
+
+
 def solution(mesh):
     return jax.shard_map(
         per_device,

time: 110 us -> 45.1 us (0.41)
  Pallas kernels: 0 us -> 39.2 us
  waiting for transfers between devices: 38.7 us -> 0 us
  blocking collectives: 27.4 us -> 0 us
  matrix products: 18.7 us -> 0 us
  between operations: 14.1 us -> 0.64 us
  starting transfers between devices: 5.57 us -> 0 us
  local copies, waits for them, and re-layouts: 1.95 us -> 5.04 us
  other arithmetic: 2.95 us -> 0 us
    pallas_call x0 -> x1, Pallas kernels: none -> 39.2 us  [fused(): pl.pallas_call(fused_kernel, out_shape=(jax.ShapeDtypeStruct((tokens, wid...]
    reduce_scatter x1 -> x0, waiting for transfers between devices: 22.6 us -> none  [per_device(): lax.psum_scatter(lax.dot_general(columns, hidden[0], (((0,), (1,)), ((),...]
    all_to_all x1 -> x0, blocking collectives: 21 us -> none  [per_device(): lax.all_to_all(to_send, 'expert', split_axis=1, concat_axis=1, tiled=True)]
    dot_general x4 -> x0, matrix products: 18.7 us -> none  [the longest x1 8.76 us: per_device(): lax.dot_general(columns, hidden[0], (((0,), (1,)), ((), ())), preferred_e...]
    all_gather x1 -> x0, waiting for transfers between devices: 16 us -> none  [per_device(): lax.all_gather(arrived, 'tensor', axis=0, tiled=True)]
    psum x1 -> x0, blocking collectives: 6.4 us -> none  [per_device(): gate_grad = lax.psum(own_terms, 'tensor')]
    all_to_all x1 -> x0, starting transfers between devices: 5.49 us -> none  [per_device(): lax.all_to_all(outgoing, 'expert', split_axis=1, concat_axis=1, tiled=True)]
    unnamed x9 -> x3, local copies, waits for them, and re-layouts: 1.25 us -> 5.04 us
  transfers between devices with their start and end apart: 3 -> 0, of which waited for: 2 -> 0; matrix products, arithmetic and copies ran while one was open for 11% -> 0% of each run, Pallas kernels for 0% -> 0%
where the time goes in v1:
time: 45.1 us; the launch traced here: 44.9 us
  Pallas kernels  39.2 us (87%)
  local copies, waits for them, and re-layouts  5.04 us (11%)
  between operations  0.64 us (1%)
    pallas_call x1, Pallas kernels, fused(): pl.pallas_call(fused_kernel, out_shape=(jax.ShapeDtypeStruct((tokens, wid...  39.2 us
    unnamed x3, local copies, waits for them, and re-layouts  5.04 us

profile of v1, /device:TPU:0, one launch (start us, length us, event | category | flops | bytes accessed | tf_op | source)
XLA Modules:
  0.0 44.9 jit_solution(5788757477934932068)
XLA Ops:
  0.6 39.2 %shard_map.76 = (bf16[128,768]{1,0:T(8,128)(2,1)}, f32[2,128]{1,0:T(2,128)}, bf16[1,320,1536]{2,1,0:T(8,128)(2,1)}) custom-call(s32[2,128]{1,0:T(2,128)} %bitcast.4, f32[2,128]{1,0:T(2,128)} %bitcast.5, bf16[128,768]{1,0:T(8,128)(2,1)} %out_grad_ref.1, bf16[1,320,1536]{2,1,0:T(8,128)(2,1)} %hidden_hbm.1, bf16[1,1536,3072]{2,1,0:T(8,128)(2,1)} %weight_hbm.1), custom_call_target="tpu_custom_call" | custom-call | flops 6039797760 | bytes 9437184 | tf_op jit(solution)/shard_map/pallas_call | solution.py:250
  39.9 1.6 %copy.11 = bf16[128,768]{1,0:T(8,128)(2,1)} copy(bf16[128,768]{1,0:T(8,128)(2,1)} %get-tuple-element.12) | data formatting | bytes 393216
  41.5 1.2 %copy.12 = f32[128,2]{0,1:T(2,128)} copy(f32[128,2]{0,1:T(2,128)} %bitcast.3) | data formatting | bytes 2048
  42.7 2.2 %copy.13 = bf16[1,320,1536]{2,1,0:T(8,128)(2,1)} copy(bf16[1,320,1536]{2,1,0:T(8,128)(2,1)} %get-tuple-element.14) | data formatting | bytes 1966080

commit v2 on v1

--- a/solution.py
+++ b/solution.py
@@ -6,8 +6,8 @@
 from jax.sharding import PartitionSpec as P
 
 BF16, F32 = jnp.bfloat16, jnp.float32
-FAR_FIRST = (4, 3, 5, 2, 6, 1, 7, 0)
-NEAR_FIRST = (0, 1, 7, 2, 6, 3, 5, 4)
+FAR_FIRST = (4, 5, 6, 7, 2, 3, 1, 0)
+NEAR_FIRST = (0, 1, 2, 3, 6, 7, 4, 5)
 
 
 def plain(routes, gate_weights, out_grad, hidden, down_weight):
@@ -76,6 +76,13 @@
     diagonal = (1 - chip) * 2 + (1 - core)
     width = 2 * half
 
+    def partner(i):
+        index = own
+        for bit in (1, 2, 4):
+            if i & bit:
+                index = index + bit * (1 - 2 * ((own // bit) % 2))
+        return index
+
     def send(source, target, send_sem, recv_sem, expert, tensor):
         return pltpu.make_async_remote_copy(
             src_ref=source, dst_ref=target, send_sem=send_sem, recv_sem=recv_sem,
@@ -92,7 +99,7 @@
 
     barrier = pltpu.get_barrier_semaphore()
     for i in range(1, experts):
-        pl.semaphore_signal(barrier, inc=1, device_id=((own + i) % experts, rank),
+        pl.semaphore_signal(barrier, inc=1, device_id=(partner(i), rank),
                             device_id_type=pl.DeviceIdType.MESH)
     for peer in (sibling, across, diagonal):
         pl.semaphore_signal(barrier, inc=1, device_id=(own, peer),
@@ -132,41 +139,16 @@
     sends = []
     token_copies = {}
     for i in FAR_FIRST[:-1]:
-        expert = (own + i) % experts
+        expert = partner(i)
         token_copies[i] = send(tokens_out.at[expert], gathered.at[0, own],
                                tok_send.at[i], tok_recv.at[i], expert, rank)
         token_copies[i].start()
     gathered[0, own] = tokens_out[own]
 
-    def product(j):
-        return pack(jnp.dot(hidden[...], weight[j], preferred_element_type=F32))
-
-    loads[0].wait()
-    loads[1].wait()
-    core_out[0] = product(0).astype(BF16)
-    to_core = [send(core_out.at[n], core_in.at[n], core_send.at[n], core_recv.at[n], own, sibling)
-               for n in range(2)]
-    to_core[0].start()
-    loads[2].wait()
-    partial[...] = product(1)
-    to_core[0].wait_recv()
-    to_y = {}
-    for i in FAR_FIRST:
-        expert = (own + i) % experts
-        y_out[expert] = (partial[expert] + core_in[0, expert].astype(F32)).astype(BF16)
-        to_y[i] = send(y_out.at[expert], y_in.at[expert], y_send.at[i], y_recv.at[i], own, across)
-        to_y[i].start()
-    loads[3].wait()
-    core_out[1] = product(2).astype(BF16)
-    to_core[1].start()
-    loads[4].wait()
-    partial[...] = product(3)
-    to_core[1].wait_recv()
-    partial[...] = partial[...] + core_in[1].astype(F32)
-
     to_slots, to_sibling, to_across, onward = {}, {}, {}, {}
-    for far, near in zip(FAR_FIRST, NEAR_FIRST):
-        source = (own - near + experts) % experts
+
+    def share(near):
+        source = partner(near)
         if near:
             token_copies[near].wait_recv()
         to_across[near] = send(gathered.at[0, source], gathered.at[2, source],
@@ -176,7 +158,39 @@
                                 gc_send.at[near], gc_recv.at[near], own, sibling)
         to_sibling[near].start()
 
-        expert = (own + far) % experts
+    share(0)
+
+    def product(j):
+        return pack(jnp.dot(hidden[...], weight[j], preferred_element_type=F32))
+
+    loads[0].wait()
+    loads[1].wait()
+    core_out[0] = product(0).astype(BF16)
+    to_core = [send(core_out.at[n], core_in.at[n], core_send.at[n], core_recv.at[n], own, sibling)
+               for n in range(2)]
+    to_core[0].start()
+    share(1)
+    loads[2].wait()
+    partial[...] = product(1)
+    share(2)
+    to_core[0].wait_recv()
+    to_y = {}
+    for i in FAR_FIRST:
+        expert = partner(i)
+        y_out[expert] = (partial[expert] + core_in[0, expert].astype(F32)).astype(BF16)
+        to_y[i] = send(y_out.at[expert], y_in.at[expert], y_send.at[i], y_recv.at[i], own, across)
+        to_y[i].start()
+    loads[3].wait()
+    core_out[1] = product(2).astype(BF16)
+    to_core[1].start()
+    share(3)
+    loads[4].wait()
+    partial[...] = product(3)
+    to_core[1].wait_recv()
+    partial[...] = partial[...] + core_in[1].astype(F32)
+
+    for step, far in enumerate(FAR_FIRST):
+        expert = partner(far)
         to_y[far].wait_recv()
         block = (partial[expert] + y_in[expert].astype(F32)).astype(BF16)
         if far:
@@ -186,6 +200,8 @@
             to_slots[far].start()
         else:
             returned[own] = block
+        if step % 2:
+            share(NEAR_FIRST[4 + step // 2])
 
     def back(part, j):
         return lax.dot_general(unpack(gathered[part]), weight[j], (((1,), (1,)), ((), ())),
@@ -196,7 +212,7 @@
         to_sibling[near].wait_recv()
     total[...] = total[...] + back(1, 2)
     for near in NEAR_FIRST:
-        source = (own - near + experts) % experts
+        source = partner(near)
         to_across[near].wait_recv()
         onward[near] = send(gathered.at[2, source], gathered.at[3, source],
                             gf_send.at[near], gf_recv.at[near], own, sibling)
@@ -239,6 +255,23 @@
         copy.wait_send()
 
 
+def hand_over_kernel(layer_in, gate_in, grad_in, layer_ref, gate_ref, grad_ref):
+    layer_ref[...] = layer_in[...]
+    gate_ref[...] = gate_in[...]
+    grad_ref[...] = grad_in[...]
+
+
+def hand_over(*arrays):
+    vmem = pl.BlockSpec(memory_space=pltpu.VMEM)
+    return pl.pallas_call(
+        hand_over_kernel,
+        out_shape=tuple(jax.ShapeDtypeStruct(a.shape, a.dtype) for a in arrays),
+        in_specs=[vmem] * 3,
+        out_specs=(vmem,) * 3,
+        compiler_params=pltpu.CompilerParams(vmem_limit_bytes=16 * 1024 * 1024),
+    )(*arrays)
+
+
 def fused(routes, gate_weights, out_grad, hidden, down_weight):
     experts = lax.axis_size("expert")
     _, slots, depth = hidden.shape
@@ -273,12 +306,13 @@
             sems(5), sems(2), sems(2),
         ] + [sems(8)] * 12 + [sems(3), sems(3)],
         compiler_params=pltpu.CompilerParams(
-            collective_id=0, has_side_effects=True, vmem_limit_bytes=56 * 1024 * 1024
+            collective_id=0, has_side_effects=True, vmem_limit_bytes=52 * 1024 * 1024
         ),
         cost_estimate=pl.CostEstimate(
             flops=16 * slots * depth * width, bytes_accessed=8 * depth * width, transcendentals=0
         ),
     )(routes.T, gate_weights.T, out_grad, hidden, down_weight)
+    layer_out, gate_grad, hidden_grad = hand_over(layer_out, gate_grad, hidden_grad)
     return layer_out, gate_grad.T, hidden_grad
 
 

time: 45.1 us -> 40.7 us (0.902)
  the two profiles are of different devices: /device:TPU:0 before, /device:TPU:9 now
where the time goes in v2:
time: 40.7 us; the launch traced here: 40.6 us
  Pallas kernels  37.6 us (92%)
  local copies, waits for them, and re-layouts  2.28 us (6%)
  between operations  0.65 us (2%)
    pallas_call x1, Pallas kernels, fused(): pl.pallas_call(fused_kernel, out_shape=(jax.ShapeDtypeStruct((tokens, wid...  36.6 us
    unnamed x6, local copies, waits for them, and re-layouts  2.28 us
    pallas_call x1, Pallas kernels, hand_over(): pl.pallas_call(hand_over_kernel, out_shape=tuple((jax.ShapeDtypeStruct(a....  1.09 us

profile of v2, /device:TPU:9, one launch (start us, length us, event | category | flops | bytes accessed | tf_op | source)
XLA Modules:
  0.0 40.6 jit_solution(755587482478711409)
XLA Ops:
  0.6 0.0 copy-start
  0.6 0.9 %copy-done = bf16[128,768]{1,0:T(8,128)(2,1)S(1)} copy-done((bf16[128,768]{1,0:T(8,128)(2,1)S(1)}, bf16[128,768]{1,0:T(8,128)(2,1)}, u32[]{:S(2)}) %copy-start) | copy-done | bytes 196632
  1.6 0.0 copy-start.1
  1.6 0.7 %copy-done.1 = s32[128,2]{0,1:T(2,128)S(1)} copy-done((s32[128,2]{0,1:T(2,128)S(1)}, s32[128,2]{0,1:T(2,128)}, u32[]{:S(2)}) %copy-start.1) | copy-done | bytes 1048
  2.2 0.0 copy-start.2
  2.2 0.7 %copy-done.2 = f32[128,2]{0,1:T(2,128)S(1)} copy-done((f32[128,2]{0,1:T(2,128)S(1)}, f32[128,2]{0,1:T(2,128)}, u32[]{:S(2)}) %copy-start.2) | copy-done | bytes 1048
  2.9 36.6 %shard_map.76 = (bf16[128,768]{1,0:T(8,128)(2,1)S(1)}, f32[2,128]{1,0:T(2,128)S(1)}, bf16[1,320,1536]{2,1,0:T(8,128)(2,1)S(1)}) custom-call(s32[2,128]{1,0:T(2,128)S(1)} %bitcast.3, f32[2,128]{1,0:T(2,128)S(1)} %bitcast.4, bf16[128,768]{1,0:T(8,128)(2,1)S(1)} %copy-done, bf16[1,320,1536]{2,1,0:T(8,128)(2,1)} %hidden_hbm.1, bf16[1,1536,3072]{2,1,0:T(8,128)(2,1)} %weight_hbm.1), custom_call_target="tpu_custom_call" | custom-call | flops 6039797760 | bytes 9437184 | tf_op jit(solution)/shard_map/pallas_call | solution.py:283
  39.5 1.1 %shard_map.77 = (bf16[128,768]{1,0:T(8,128)(2,1)}, f32[2,128]{1,0:T(2,128)}, bf16[1,320,1536]{2,1,0:T(8,128)(2,1)}) custom-call(bf16[128,768]{1,0:T(8,128)(2,1)S(1)} %get-tuple-element.9.layer_in, f32[2,128]{1,0:T(2,128)S(1)} %get-tuple-element.10.gate_in, bf16[1,320,1536]{2,1,0:T(8,128)(2,1)S(1)} %get-tuple-element.11.grad_in), custom_call_target="tpu_custom_call" | custom-call | tf_op jit(solution)/shard_map/pallas_call | solution.py:266
Async XLA Ops:
  0.6 0.9 %copy-start = (bf16[128,768]{1,0:T(8,128)(2,1)S(1)}, bf16[128,768]{1,0:T(8,128)(2,1)}, u32[]{:S(2)}) copy-start(bf16[128,768]{1,0:T(8,128)(2,1)} %out_grad_ref.1) | copy-start | bytes 589828
  1.6 0.7 %copy-start.1 = (s32[128,2]{0,1:T(2,128)S(1)}, s32[128,2]{0,1:T(2,128)}, u32[]{:S(2)}) copy-start(s32[128,2]{0,1:T(2,128)} %param.5) | copy-start | bytes 3076
  2.2 0.7 %copy-start.2 = (f32[128,2]{0,1:T(2,128)S(1)}, f32[128,2]{0,1:T(2,128)}, u32[]{:S(2)}) copy-start(f32[128,2]{0,1:T(2,128)} %param.6) | copy-start | bytes 3076

commit v3 on v2

--- a/solution.py
+++ b/solution.py
@@ -94,7 +94,7 @@
         columns = pl.ds(pl.multiple_of(group * width, width), width)
         loads.append(pltpu.make_async_copy(
             weight_hbm.at[0, :, columns], weight.at[j], load_sem.at[j]))
-    for load in loads:
+    for load in loads[:2]:
         load.start()
 
     barrier = pltpu.get_barrier_semaphore()
@@ -133,6 +133,9 @@
     picked = jnp.dot((marks[0] + marks[1]).astype(BF16), out_grad_ref[...],
                      preferred_element_type=F32)
     tokens_out[...] = pack(picked * slot_gate).astype(BF16)
+
+    for load in loads[2:]:
+        load.start()
 
     pl.semaphore_wait(barrier, experts - 1 + 3)
 
@@ -211,13 +214,16 @@
     for near in NEAR_FIRST:
         to_sibling[near].wait_recv()
     total[...] = total[...] + back(1, 2)
-    for near in NEAR_FIRST:
+
+    def pass_on(near):
         source = partner(near)
         to_across[near].wait_recv()
         onward[near] = send(gathered.at[2, source], gathered.at[3, source],
                             gf_send.at[near], gf_recv.at[near], own, sibling)
         onward[near].start()
-    total[...] = total[...] + back(2, 1)
+
+    for near in NEAR_FIRST[:6]:
+        pass_on(near)
 
     for far in FAR_FIRST[:-1]:
         to_slots[far].wait_recv()
@@ -240,6 +246,9 @@
                              own, peer))
         to_terms[n].start()
 
+    for near in NEAR_FIRST[6:]:
+        pass_on(near)
+    total[...] = total[...] + back(2, 1)
     for near in NEAR_FIRST:
         onward[near].wait_recv()
     hidden_grad_ref[0] = (total[...] + back(3, 0)).astype(BF16)

time: 40.7 us -> 39.2 us (0.963)
  Pallas kernels: 37.6 us -> 36.1 us
    pallas_call x1, Pallas kernels: 36.6 us -> 35 us  [fused(): pl.pallas_call(fused_kernel, out_shape=(jax.ShapeDtypeStruct((tokens, wid...]
where the time goes in v3:
time: 39.2 us; the launch traced here: 39 us
  Pallas kernels  36.1 us (92%)
  local copies, waits for them, and re-layouts  2.28 us (6%)
  between operations  0.65 us (2%)
    pallas_call x1, Pallas kernels, fused(): pl.pallas_call(fused_kernel, out_shape=(jax.ShapeDtypeStruct((tokens, wid...  35 us
    unnamed x6, local copies, waits for them, and re-layouts  2.28 us
    pallas_call x1, Pallas kernels, hand_over(): pl.pallas_call(hand_over_kernel, out_shape=tuple((jax.ShapeDtypeStruct(a....  1.09 us

profile of v3, /device:TPU:9, one launch (start us, length us, event | category | flops | bytes accessed | tf_op | source)
XLA Modules:
  0.0 39.0 jit_solution(8287223145045277729)
XLA Ops:
  0.6 0.0 copy-start
  0.6 0.9 %copy-done = bf16[128,768]{1,0:T(8,128)(2,1)S(1)} copy-done((bf16[128,768]{1,0:T(8,128)(2,1)S(1)}, bf16[128,768]{1,0:T(8,128)(2,1)}, u32[]{:S(2)}) %copy-start) | copy-done | bytes 196632
  1.6 0.0 copy-start.1
  1.6 0.7 %copy-done.1 = s32[128,2]{0,1:T(2,128)S(1)} copy-done((s32[128,2]{0,1:T(2,128)S(1)}, s32[128,2]{0,1:T(2,128)}, u32[]{:S(2)}) %copy-start.1) | copy-done | bytes 1048
  2.2 0.0 copy-start.2
  2.2 0.7 %copy-done.2 = f32[128,2]{0,1:T(2,128)S(1)} copy-done((f32[128,2]{0,1:T(2,128)S(1)}, f32[128,2]{0,1:T(2,128)}, u32[]{:S(2)}) %copy-start.2) | copy-done | bytes 1048
  2.9 35.0 %shard_map.76 = (bf16[128,768]{1,0:T(8,128)(2,1)S(1)}, f32[2,128]{1,0:T(2,128)S(1)}, bf16[1,320,1536]{2,1,0:T(8,128)(2,1)S(1)}) custom-call(s32[2,128]{1,0:T(2,128)S(1)} %bitcast.3, f32[2,128]{1,0:T(2,128)S(1)} %bitcast.4, bf16[128,768]{1,0:T(8,128)(2,1)S(1)} %copy-done, bf16[1,320,1536]{2,1,0:T(8,128)(2,1)} %hidden_hbm.1, bf16[1,1536,3072]{2,1,0:T(8,128)(2,1)} %weight_hbm.1), custom_call_target="tpu_custom_call" | custom-call | flops 6039797760 | bytes 9437184 | tf_op jit(solution)/shard_map/pallas_call | solution.py:292
  37.9 1.1 %shard_map.77 = (bf16[128,768]{1,0:T(8,128)(2,1)}, f32[2,128]{1,0:T(2,128)}, bf16[1,320,1536]{2,1,0:T(8,128)(2,1)}) custom-call(bf16[128,768]{1,0:T(8,128)(2,1)S(1)} %get-tuple-element.9.layer_in, f32[2,128]{1,0:T(2,128)S(1)} %get-tuple-element.10.gate_in, bf16[1,320,1536]{2,1,0:T(8,128)(2,1)S(1)} %get-tuple-element.11.grad_in), custom_call_target="tpu_custom_call" | custom-call | tf_op jit(solution)/shard_map/pallas_call | solution.py:275
Async XLA Ops:
  0.6 0.9 %copy-start = (bf16[128,768]{1,0:T(8,128)(2,1)S(1)}, bf16[128,768]{1,0:T(8,128)(2,1)}, u32[]{:S(2)}) copy-start(bf16[128,768]{1,0:T(8,128)(2,1)} %out_grad_ref.1) | copy-start | bytes 589828
  1.6 0.7 %copy-start.1 = (s32[128,2]{0,1:T(2,128)S(1)}, s32[128,2]{0,1:T(2,128)}, u32[]{:S(2)}) copy-start(s32[128,2]{0,1:T(2,128)} %param.5) | copy-start | bytes 3076
  2.2 0.7 %copy-start.2 = (f32[128,2]{0,1:T(2,128)S(1)}, f32[128,2]{0,1:T(2,128)}, u32[]{:S(2)}) copy-start(f32[128,2]{0,1:T(2,128)} %param.6) | copy-start | bytes 3076

commit v4 on v3

--- a/solution.py
+++ b/solution.py
@@ -175,7 +175,6 @@
     share(1)
     loads[2].wait()
     partial[...] = product(1)
-    share(2)
     to_core[0].wait_recv()
     to_y = {}
     for i in FAR_FIRST:
@@ -183,6 +182,7 @@
         y_out[expert] = (partial[expert] + core_in[0, expert].astype(F32)).astype(BF16)
         to_y[i] = send(y_out.at[expert], y_in.at[expert], y_send.at[i], y_recv.at[i], own, across)
         to_y[i].start()
+    share(2)
     loads[3].wait()
     core_out[1] = product(2).astype(BF16)
     to_core[1].start()

time: 39.2 us -> 37.6 us (0.959)
  the two profiles are of different devices: /device:TPU:9 before, /device:TPU:0 now
where the time goes in v4:
time: 37.6 us; the launch traced here: 37.4 us
  Pallas kernels  34.5 us (92%)
  local copies, waits for them, and re-layouts  2.28 us (6%)
  between operations  0.65 us (2%)
    pallas_call x1, Pallas kernels, fused(): pl.pallas_call(fused_kernel, out_shape=(jax.ShapeDtypeStruct((tokens, wid...  33.4 us
    unnamed x6, local copies, waits for them, and re-layouts  2.28 us
    pallas_call x1, Pallas kernels, hand_over(): pl.pallas_call(hand_over_kernel, out_shape=tuple((jax.ShapeDtypeStruct(a....  1.09 us

profile of v4, /device:TPU:0, one launch (start us, length us, event | category | flops | bytes accessed | tf_op | source)
XLA Modules:
  0.0 37.4 jit_solution(14721956749724493255)
XLA Ops:
  0.6 0.0 copy-start
  0.6 0.9 %copy-done = bf16[128,768]{1,0:T(8,128)(2,1)S(1)} copy-done((bf16[128,768]{1,0:T(8,128)(2,1)S(1)}, bf16[128,768]{1,0:T(8,128)(2,1)}, u32[]{:S(2)}) %copy-start) | copy-done | bytes 196632
  1.6 0.0 copy-start.1
  1.6 0.7 %copy-done.1 = s32[128,2]{0,1:T(2,128)S(1)} copy-done((s32[128,2]{0,1:T(2,128)S(1)}, s32[128,2]{0,1:T(2,128)}, u32[]{:S(2)}) %copy-start.1) | copy-done | bytes 1048
  2.2 0.0 copy-start.2
  2.2 0.7 %copy-done.2 = f32[128,2]{0,1:T(2,128)S(1)} copy-done((f32[128,2]{0,1:T(2,128)S(1)}, f32[128,2]{0,1:T(2,128)}, u32[]{:S(2)}) %copy-start.2) | copy-done | bytes 1048
  2.9 33.4 %shard_map.76 = (bf16[128,768]{1,0:T(8,128)(2,1)S(1)}, f32[2,128]{1,0:T(2,128)S(1)}, bf16[1,320,1536]{2,1,0:T(8,128)(2,1)S(1)}) custom-call(s32[2,128]{1,0:T(2,128)S(1)} %bitcast.3, f32[2,128]{1,0:T(2,128)S(1)} %bitcast.4, bf16[128,768]{1,0:T(8,128)(2,1)S(1)} %copy-done, bf16[1,320,1536]{2,1,0:T(8,128)(2,1)} %hidden_hbm.1, bf16[1,1536,3072]{2,1,0:T(8,128)(2,1)} %weight_hbm.1), custom_call_target="tpu_custom_call" | custom-call | flops 6039797760 | bytes 9437184 | tf_op jit(solution)/shard_map/pallas_call | solution.py:292
  36.3 1.1 %shard_map.77 = (bf16[128,768]{1,0:T(8,128)(2,1)}, f32[2,128]{1,0:T(2,128)}, bf16[1,320,1536]{2,1,0:T(8,128)(2,1)}) custom-call(bf16[128,768]{1,0:T(8,128)(2,1)S(1)} %get-tuple-element.9.layer_in, f32[2,128]{1,0:T(2,128)S(1)} %get-tuple-element.10.gate_in, bf16[1,320,1536]{2,1,0:T(8,128)(2,1)S(1)} %get-tuple-element.11.grad_in), custom_call_target="tpu_custom_call" | custom-call | tf_op jit(solution)/shard_map/pallas_call | solution.py:275
Async XLA Ops:
  0.6 0.9 %copy-start = (bf16[128,768]{1,0:T(8,128)(2,1)S(1)}, bf16[128,768]{1,0:T(8,128)(2,1)}, u32[]{:S(2)}) copy-start(bf16[128,768]{1,0:T(8,128)(2,1)} %out_grad_ref.1) | copy-start | bytes 589828
  1.6 0.7 %copy-start.1 = (s32[128,2]{0,1:T(2,128)S(1)}, s32[128,2]{0,1:T(2,128)}, u32[]{:S(2)}) copy-start(s32[128,2]{0,1:T(2,128)} %param.5) | copy-start | bytes 3076
  2.2 0.7 %copy-start.2 = (f32[128,2]{0,1:T(2,128)S(1)}, f32[128,2]{0,1:T(2,128)}, u32[]{:S(2)}) copy-start(f32[128,2]{0,1:T(2,128)} %param.6) | copy-start | bytes 3076
